TPU v7x, 32 devices: a whole 2x2x4 slice. The times are simulated.
32 devices in a mesh: batch: 4 (over x, core), mp: 8 (over z, y).
Axes of the slice: x: 2, y: 2, z: 4, core: 2. Of those that a mesh axis runs over, the one named last changes fastest.
Arguments:
- features: bfloat16 [2, 6144, 9216], P(None, 'batch', 'mp'), may hold values from -6 to 6
- weights: bfloat16 [2, 9216, 4096], P(None, None, 'mp'), may hold values from -0.0625 to 0.0625
- bias: float32 [2, 4096], P(None, 'mp'), may hold values from -3 to 3
- stitch: float32 [2, 2, 4096], P(None, None, 'mp'), may hold values from 0.1 to 1
- cotangent: bfloat16 [2, 6144, 4096], P(None, 'batch', 'mp'), may hold values from -84 to 84
- crop_counts: int32 [256], P('batch'), may hold values from 1 to 47
- row_mask: int32 [6144], P('batch'), may hold values 0 or 1
- flags: int32 [2, 2, 8], replicated, may hold values from 0 to 1
Outputs:
- mixed: bfloat16 [2, 6144, 4096], P(None, 'batch', 'mp')
- grad_features: bfloat16 [2, 6144, 9216], P(None, 'batch', 'mp')
- grad_weights: float32 [2, 9216, 4096], P(None, None, 'mp')
- grad_bias: float32 [2, 4096], P(None, 'mp')
- grad_stitch: float32 [2, 2, 4096], P(None, None, 'mp')
All inputs are finite; a program needn't handle non-finite values. No bound on the sum of `row_mask` on one device may be relied on, other than what follows from the above.
Results may differ from a plain program's by a relative error of at most 0.0049.
Values may be sent and summed in bfloat16 or wider, within the bound.
A program may use at most 448 MiB of HBM per device.

v0:
```python
import collections
import functools

import jax
import jax.numpy as jnp
from jax import lax
from jax.experimental import pallas as pl
from jax.experimental.pallas import tpu as pltpu
from jax.sharding import PartitionSpec as P

FLAG_GROUPS = 8
OUTER = 4


def row_weights(counts, mask):
    ends = jnp.cumsum(counts)
    starts = ends - counts
    index = lax.broadcasted_iota(jnp.int32, (mask.shape[0], counts.shape[0]), 0)
    inside = (index >= starts[None, :]) & (index < ends[None, :])
    count_row = jnp.sum(jnp.where(inside, counts[None, :], 0), axis=1)
    live = (count_row > 0) & (mask == 1)
    return jnp.where(live, 1.0 / jnp.maximum(count_row, 1).astype(jnp.float32), 0.0)


def project_bias(task_bias, flags):
    local_width = task_bias.shape[2]
    channel = lax.axis_index("mp") * local_width + lax.broadcasted_iota(
        jnp.int32, (local_width, FLAG_GROUPS), 0
    )
    member = (
        channel % FLAG_GROUPS == lax.broadcasted_iota(jnp.int32, (local_width, FLAG_GROUPS), 1)
    ).astype(jnp.float32)
    dots = jnp.dot(task_bias[0] * task_bias[1], member, precision=lax.Precision.HIGHEST)
    norms = jnp.einsum(
        "stc,cg->stg", task_bias * task_bias, member, precision=lax.Precision.HIGHEST
    )
    dots, norms = lax.psum((dots, norms), "mp")
    flag = flags.astype(jnp.float32)
    coef_first = jnp.dot(
        flag[0] * dots / (norms[1] + 1e-06), member.T, precision=lax.Precision.HIGHEST
    )
    coef_second = jnp.dot(
        flag[1] * dots / (norms[0] + 1e-06), member.T, precision=lax.Precision.HIGHEST
    )
    first = task_bias[0] - coef_first * task_bias[1]
    second = task_bias[1] - coef_second * task_bias[0]
    return first + second


def generic_plan(mesh):
    n_mp = mesh.shape["mp"]
    n_batch = mesh.shape["batch"]
    inner = n_mp // OUTER
    inner_groups = [[o * inner + i for i in range(inner)] for o in range(OUTER)]
    outer_groups = [[o * inner + i for o in range(OUTER)] for i in range(inner)]

    def per_device(features, weights, bias, stitch, cotangent, crop_counts, row_mask, flags):
        rows = features.shape[1]
        width = weights.shape[2]
        depth = features.shape[2] * inner
        held = lax.all_gather(
            features, "mp", axis=2, tiled=True, axis_index_groups=inner_groups
        )
        split = weights.reshape(2, OUTER, depth, width)
        block = lax.all_to_all(
            split, "mp", split_axis=1, concat_axis=1, axis_index_groups=outer_groups
        )
        block = block.reshape(2, OUTER, depth, width)
        part = jnp.einsum("trk,tokc->otrc", held, block, preferred_element_type=jnp.float32)
        linear = lax.psum_scatter(
            part.astype(jnp.bfloat16),
            "mp",
            scatter_dimension=0,
            axis_index_groups=outer_groups,
        ).astype(jnp.float32)
        pre = linear + bias[:, None, :]
        hidden, gelu_back = jax.vjp(lambda v: jax.nn.gelu(v, approximate=False), pre)
        mixed = stitch[:, 0, None, :] * hidden[0][None] + stitch[:, 1, None, :] * hidden[1][None]
        scale_rows = row_weights(crop_counts, row_mask)
        grad_out = cotangent.astype(jnp.float32) * scale_rows[None, :, None]
        first_task = gelu_back(stitch[0][:, None, :] * grad_out[0][None])[0]
        second_task = gelu_back(stitch[1][:, None, :] * grad_out[1][None])[0]
        task_bias = jnp.stack([jnp.sum(first_task, axis=1), jnp.sum(second_task, axis=1)])
        grad_linear = (first_task + second_task).astype(jnp.bfloat16)
        grad_stitch = jnp.sum(grad_out[:, None] * hidden[None], axis=2)
        every = lax.all_gather(grad_linear, "mp", axis_index_groups=outer_groups)
        grad_part = jnp.einsum(
            "otrc,tokc->trk", every, block, preferred_element_type=jnp.float32
        )
        grad_part = grad_part.astype(jnp.bfloat16).reshape(2, rows, inner, depth // inner)
        grad_features = lax.psum_scatter(
            grad_part.transpose(2, 0, 1, 3),
            "mp",
            scatter_dimension=0,
            axis_index_groups=inner_groups,
        )
        weight_part = jnp.einsum(
            "trk,otrc->otkc", held, every, preferred_element_type=jnp.float32
        )
        weight_part = weight_part.astype(jnp.bfloat16).reshape(
            OUTER, 2, n_batch, depth // n_batch, width
        )
        share = lax.psum_scatter(
            weight_part.transpose(2, 0, 1, 3, 4), "batch", scatter_dimension=0
        )
        share = lax.all_to_all(
            share, "mp", split_axis=0, concat_axis=0, axis_index_groups=outer_groups
        )
        share = share.reshape(OUTER, 2, depth // n_batch, width)
        whole = lax.all_gather(share, "batch")
        grad_weights = whole.transpose(2, 1, 0, 3, 4).reshape(2, OUTER * depth, width)
        task_bias, grad_stitch = lax.psum((task_bias, grad_stitch), "batch")
        grad_bias = project_bias(task_bias, flags)
        return (
            mixed.astype(jnp.bfloat16),
            grad_features.astype(jnp.bfloat16),
            grad_weights.astype(jnp.float32),
            grad_bias,
            grad_stitch,
        )

    return per_device


MESH = pl.DeviceIdType.MESH
BF16 = jnp.bfloat16
F32 = jnp.float32
ZED = 4
HALVES = 2
PHASES = 4
RING = 8
BAND = 32
SUB = 2
PRODUCTS = 6
HELD = 4
WIDEN_BLOCKS = 18
WIDEN_SLOTS = 6

DX_TIMES = (20, 21, 23, 25, 27, 29, 43, 45, 48, 50, 58, 64)
DX_BEGINS = (22, 24, 26, 28, 30, 34, 44, 48, 57, 60, 68, 76)
DX_ENDS = (23, 25, 27, 29, 31, 43, 45, 50, 59, 62, 71, 81)
ONES = (19, 23, 26, 30, 33, 40, 43, 45, 46, 54, 56, 57)
TWOS = (22, 26, 27, 32, 36, 42, 44, 46, 49, 55, 57, 61)
THREES = (23, 28, 33, 35, 42, 43, 45, 52, 55, 58, 59, 70)
FOURS = (25, 30, 35, 37, 44, 47, 50, 54, 60, 67, 68, 73)
FIVES = (33, 36, 44, 45, 51, 59, 62, 67, 74, 76, 82, 85)
SIXES = (35, 43, 47, 57, 64, 70, 75, 82, 84, 86, 87, 90)
W_STRIPS = {2: (5, 7, 8, 11, 12, 13), 3: (21, 22, 23, 24, 26, 27)}
W_ACROSS = {1: (0, 0, 2), 2: (16, 21, 22), 3: (29, 29, 34)}
W_CORES = {1: (1, 6, 7), 2: (21, 23, 23), 3: (33, 33, 35)}


Part = collections.namedtuple("Part", ("u", "p", "i", "t", "h", "slot", "prod", "buf"))
Tile = collections.namedtuple("Tile", ("g", "p", "t", "h", "j", "buf", "trio", "quad"))


def half(value):
    return value.astype(BF16)


def wide(value):
    return value.astype(F32)


def fused_kernel(
    rows, deep, width, chunk,
    feat, wts, cot, bias, stitch, counts, mask, flags,
    mixed, gfeat, gwt, gbias, gstitch, xn, dxn,
    wv, gl, rs, h0, xc, pf, cc, mx, own, dsend, dfetch, dout,
    xsrc, xt, cstage, cland, xstage, xland, kept, zstage,
    scale, stat, sums, sums_land, prods, prods_land,
    rs_send, rs_recv, ag_send, ag_recv, xs_send, xs_recv,
    wz_send, wz_recv, wx_send, wx_recv, wc_send, wc_recv, wl,
    xf, cf, mxs, dx_send, dx_recv, df, dod,
    tile_in, c_send, c_recv, x_send, x_recv, z_send, z_recv, zl, zx_send,
    ax_send, ax_recv, ac_send, ac_recv, t_send, t_recv,
):
    batch, mp = lax.axis_index("batch"), lax.axis_index("mp")
    z, y = mp // 2, mp % 2
    x, c = batch // 2, batch % 2
    up = {"mp": mp + 2}
    down = {"mp": mp - 2}
    across_y = {"mp": 2 * z + 1 - y}
    across_x = {"batch": 2 * (1 - x) + c}
    across_c = {"batch": 2 * x + 1 - c}

    def at_z(other):
        return {"mp": 2 * other + y}

    others = (3 - z, (z + 2) % 4, z + 1 - 2 * (z % 2))

    n_chunk = rows // chunk
    total = PHASES * n_chunk
    part = chunk // SUB
    n_part = rows // part
    parts = PHASES * n_part
    images = counts.shape[1]
    hw = width // HALVES
    kz = 2 * deep
    quarter = deep // 2
    tile = deep // 3
    strip = quarter // 6
    xw = hw // 2

    def mult(value, unit):
        return pl.multiple_of(value, unit)

    def remote(src, dst, send, recv, device):
        return pltpu.make_async_remote_copy(
            src_ref=src, dst_ref=dst, send_sem=send, recv_sem=recv,
            device_id=device, device_id_type=MESH,
        )

    def cols(b):
        return pl.ds(mult(b * hw, hw), hw)

    def chunk_rows(i):
        return pl.ds(mult(i * chunk, chunk), chunk)

    def part_rows(i):
        return pl.ds(mult(i * part, part), part)

    def tower(p):
        t = jnp.where(p >= HALVES, 1, 0)
        return t, p - HALVES * t

    def x_copy(t, i):
        e = t * n_chunk + i
        return remote(
            feat.at[t, chunk_rows(i)], xn.at[t, chunk_rows(i)],
            xs_send.at[e], xs_recv.at[e], across_y,
        )

    def x_fetch(t, i, buf):
        return (
            pltpu.make_async_copy(
                feat.at[t, chunk_rows(i)],
                xc.at[buf, :, pl.ds(mult(deep * y, deep), deep)], xf.at[buf, 0],
            ),
            pltpu.make_async_copy(
                xn.at[t, chunk_rows(i)],
                xc.at[buf, :, pl.ds(mult(deep * (1 - y), deep), deep)], xf.at[buf, 1],
            ),
        )

    def cot_fetch(h, i, buf):
        return pltpu.make_async_copy(
            cot.at[:, part_rows(i), cols(h)], cc.at[buf], cf.at[buf]
        )

    def w_own(p):
        t, h = tower(p)
        return pltpu.make_async_copy(
            wts.at[t, pl.ds(mult(kz * z, kz), kz), cols(h)], wv.at[p, :, cols(z)], wl.at[p],
        )

    def w_rows():
        return pl.ds(mult(deep * c + quarter * x, quarter), quarter)

    def w_z(p, to):
        t, h = tower(p)
        return remote(
            wts.at[
                t, pl.ds(mult(kz * to + deep * c + quarter * x, quarter), quarter), cols(h)
            ],
            wv.at[p, w_rows(), cols(z)],
            wz_send.at[p, to], wz_recv.at[p, z], at_z(to),
        )

    def w_z_strip(p, to, r):
        t, h = tower(p)
        at = deep * c + quarter * x + strip * r
        return remote(
            wts.at[t, pl.ds(mult(kz * to + at, strip), strip), cols(h)],
            wv.at[p, pl.ds(mult(at, strip), strip), cols(z)],
            wz_send.at[p, to], wz_recv.at[p, z], at_z(to),
        )

    def w_z_in(p, frm):
        here = wv.at[p, w_rows(), cols(frm)]
        return remote(here, here, wz_send.at[p, frm], wz_recv.at[p, frm], at_z(frm))

    def w_x(p, b):
        here = wv.at[p, w_rows(), cols(b)]
        return remote(here, here, wx_send.at[p, b], wx_recv.at[p, b], across_x)

    def w_x_in(p, b):
        here = wv.at[
            p, pl.ds(mult(deep * c + quarter * (1 - x), quarter), quarter), cols(b)
        ]
        return remote(here, here, wx_send.at[p, b], wx_recv.at[p, b], across_x)

    def w_c(p, b):
        here = wv.at[p, pl.ds(mult(deep * c, deep), deep), cols(b)]
        return remote(here, here, wc_send.at[p, b], wc_recv.at[p, b], across_c)

    def w_c_in(p, b):
        here = wv.at[p, pl.ds(mult(deep * (1 - c), deep), deep), cols(b)]
        return remote(here, here, wc_send.at[p, b], wc_recv.at[p, b], across_c)

    def rs_up(slot, zz):
        run = rs.at[slot, zz + 2 : ZED + 1]
        return remote(run, run, rs_send.at[slot, 0], rs_recv.at[slot, 0], up)

    def rs_down(slot, zz):
        run = rs.at[slot, 0:zz]
        return remote(run, run, rs_send.at[slot, 1], rs_recv.at[slot, 1], down)

    def rs_from_below(slot, zz):
        run = rs.at[slot, zz + 1 : ZED + 1]
        return remote(run, run, rs_send.at[slot, 0], rs_recv.at[slot, 0], down)

    def rs_from_above(slot, zz):
        run = rs.at[slot, 0 : zz + 1]
        return remote(run, run, rs_send.at[slot, 1], rs_recv.at[slot, 1], up)

    def at_place(first, last, do):
        for zz in range(first, last + 1):
            @pl.when(z == zz)
            def _(zz=zz):
                do(zz)

    def ag(at, b, going, device):
        here = gl.at[at.p, part_rows(at.i), cols(b)]
        return remote(
            here, here, ag_send.at[at.slot, going * ZED + b], ag_recv.at[at.slot, b], device
        )

    def dx_copy(t, i, buf):
        return remote(
            dsend.at[buf], dxn.at[t, chunk_rows(i)],
            dx_send.at[buf], dx_recv.at[t * n_chunk + i], across_y,
        )

    def dx_fetch(t, i):
        return pltpu.make_async_copy(dxn.at[t, chunk_rows(i)], dfetch, df.at[0])

    def dx_out(t, i):
        return pltpu.make_async_copy(dout, gfeat.at[t, chunk_rows(i)], dod.at[0])

    def mixed_out(h, i, buf):
        return pltpu.make_async_copy(
            mx.at[buf], mixed.at[:, part_rows(i), cols(h)], mxs.at[buf]
        )

    def tile_fetch(t, j, hk, start):
        lanes = pl.ds(mult(tile * j, tile), tile)
        near = pltpu.make_async_copy(feat.at[t, :, lanes], xsrc, tile_in.at[0])
        if not start:
            near.wait()
            return

        @pl.when(hk == y)
        def _():
            near.start()

        @pl.when(hk != y)
        def _():
            pltpu.make_async_copy(xn.at[t, :, lanes], xsrc, tile_in.at[0]).start()

    def core_copy(g):
        return remote(cstage, cland.at[g.buf], c_send.at[0], c_recv.at[g.buf], across_c)

    def across_copy(g, b):
        return remote(
            xstage.at[g.trio, b], xland.at[g.quad, b],
            x_send.at[g.trio, b], x_recv.at[g.quad, b], across_x,
        )

    def piece(g, source, core, lanes, n_lanes):
        return gwt.at[
            g.t, source,
            pl.ds(mult(deep * core + tile * g.j, tile), tile),
            pl.ds(mult(hw * g.h + lanes, xw), n_lanes),
        ]

    def z_copy(g, to):
        return remote(
            zstage.at[g.trio, to], piece(g, z, c, xw * x, xw),
            z_send.at[g.trio, to], z_recv.at[g.g, z], at_z(to),
        )

    def z_in(g, frm):
        here = piece(g, frm, c, xw * x, xw)
        return remote(here, here, z_send.at[g.trio, frm], z_recv.at[g.g, frm], at_z(frm))

    def z_own(g):
        return pltpu.make_async_copy(
            zstage.at[g.trio, z], piece(g, z, c, xw * x, xw), zl.at[g.trio]
        )

    def ax_own(g):
        return remote(
            zstage.at[g.trio, z], piece(g, z, c, xw * x, xw),
            zx_send.at[g.trio], ax_recv.at[g.g, z], across_x,
        )

    def ax_copy(g, b):
        here = piece(g, b, c, xw * x, xw)
        return remote(here, here, ax_send.at[g.g, b], ax_recv.at[g.g, b], across_x)

    def ax_in(g, b):
        here = piece(g, b, c, xw * (1 - x), xw)
        return remote(here, here, ax_send.at[g.g, b], ax_recv.at[g.g, b], across_x)

    def ac_copy(g, b):
        here = piece(g, b, c, 0, hw)
        return remote(here, here, ac_send.at[g.g, b], ac_recv.at[g.g, b], across_c)

    def ac_in(g, b):
        here = piece(g, b, 1 - c, 0, hw)
        return remote(here, here, ac_send.at[g.g, b], ac_recv.at[g.g, b], across_c)

    def sum_copy(stage, device):
        return remote(
            sums.at[stage], sums_land.at[stage], t_send.at[stage], t_recv.at[stage], device
        )

    def prod_y():
        return remote(prods.at[0], prods_land.at[ZED], t_send.at[2], t_recv.at[2], across_y)

    def prod_z(to):
        return remote(
            prods.at[1], prods_land.at[z], t_send.at[3 + to], t_recv.at[3 + z], at_z(to)
        )

    def prod_z_in(frm):
        here = prods_land.at[frm]
        return remote(here, here, t_send.at[3 + frm], t_recv.at[3 + frm], at_z(frm))

    barrier = pltpu.get_barrier_semaphore()
    for device in [at_z(o) for o in others] + [across_y, across_x, across_c]:
        pl.semaphore_signal(barrier, inc=1, device_id=device, device_id_type=MESH)
    pl.semaphore_wait(barrier, 6)

    for to in others:
        w_z(0, to).start()
    x_copy(0, 0).start()
    x_copy(0, 1).start()
    w_own(0).start()
    cot_fetch(0, 0, 0).start()

    image_row = lax.broadcasted_iota(jnp.int32, (images, images), 0)
    image_col = lax.broadcasted_iota(jnp.int32, (images, images), 1)
    crops = counts[...].astype(F32)
    ends = jnp.dot(
        jnp.broadcast_to(crops, (8, images)), (image_row <= image_col).astype(F32),
        precision=lax.Precision.HIGHEST, preferred_element_type=F32,
    )[0:1]
    starts = ends - crops
    block = mask.shape[1]
    lane = scale.shape[1]

    for r in range(rows // block):
        index = (
            lax.broadcasted_iota(jnp.int32, (block, images), 0) + r * block
        ).astype(F32)
        inside = (index >= starts) & (index < ends)
        count_row = jnp.sum(jnp.where(inside, crops, 0.0), axis=1, keepdims=True)
        diagonal = lax.broadcasted_iota(jnp.int32, (block, block), 0) == (
            lax.broadcasted_iota(jnp.int32, (block, block), 1)
        )
        usable = jnp.sum(
            jnp.where(diagonal, mask[r : r + 1, :].astype(F32), 0.0),
            axis=1, keepdims=True,
        )
        live = (count_row > 0.0) & (usable == 1.0)
        share = jnp.where(live, 1.0 / jnp.maximum(count_row, 1.0), 0.0)
        scale[r * block : (r + 1) * block, :] = jnp.broadcast_to(share, (block, lane))

    for frm in others:
        w_z_in(0, frm).wait_recv()
        w_x(0, frm).start()
    for to in others:
        w_z(1, to).start()
    w_own(1).start()
    for frm in others:
        w_x_in(0, frm).wait_recv()
        w_c(0, frm).start()
    x_copy(0, 0).wait_recv()
    for copy in x_fetch(0, 0, 0):
        copy.start()

    def final(at, later):
        p, i, slot, t, h, buf = at.p, at.i, at.slot, at.t, at.h, at.buf
        cot_fetch(h, i, buf).wait()

        @pl.when(at.u >= 2 * n_part + 2)
        def _():
            mixed_out(h, i, buf).wait()

        @pl.when(i == 0)
        def _():
            stat[p] = jnp.zeros(stat.shape[1:], F32)

        lanes = cols(h)
        shift = bias[pl.ds(t, 1), lanes]
        st = [stitch[s, pl.ds(t, 1), lanes] for s in range(2)]
        band = min(BAND, part)

        def step(r, carry):
            here = part_rows_of(r, band)
            there = pl.ds(mult(i * part + r * band, band), band)
            value = pf[at.prod, z, here, :]
            below = wide(rs[slot, z + 1, here, :])
            above = wide(rs[slot, z, here, :])
            value = value + jnp.where(z > 0, below, 0.0) + jnp.where(z < ZED - 1, above, 0.0)
            pre = value + shift
            phi = 0.5 * (1.0 + lax.erf(pre * 0.7071067811865476))
            hidden = pre * phi
            slope = phi + pre * (jnp.exp(-0.5 * pre * pre) * 0.3989422804014327)
            weight = scale[there, 0:1]
            first = wide(cc[buf, 0, here, :]) * weight
            second = wide(cc[buf, 1, here, :]) * weight
            back0 = st[0] * first * slope
            back1 = st[1] * second * slope
            gl[p, there, cols(z)] = half(back0 + back1)

            def fold(v):
                return jnp.sum(v.reshape(band // 8, 8, hw), axis=0)

            stat[p, 0] += fold(back0)
            stat[p, 1] += fold(back1)
            stat[p, 2] += fold(first * hidden)
            stat[p, 3] += fold(second * hidden)

            @pl.when(t == 0)
            def _():
                h0[h, there, :] = hidden

            @pl.when(t == 1)
            def _():
                before = h0[h, there, :]
                for s in range(2):
                    mx[buf, s, here, :] = half(
                        stitch[s, 0:1, lanes] * before + st[s] * hidden
                    )

            return carry

        lax.fori_loop(0, part // band, step, 0)

        @pl.when(z < ZED - 1)
        def _():
            ag(at, z, 0, up).start()

        @pl.when(z > 0)
        def _():
            ag(at, z, 1, down).start()

        @pl.when(t == 1)
        def _():
            mixed_out(h, i, buf).start()

        @pl.when(at.u + 1 < parts)
        def _():
            cot_fetch(later.h, later.i, later.buf).start()

    def part_rows_of(r, band):
        return pl.ds(mult(r * band, band), band)

    def forward_ag(at, far):
        @pl.when((at.u >= 0) & (at.u < parts))
        def _():
            @pl.when(z - far >= 0)
            def _():
                ag(at, z - far, 0, up).wait_recv()

                @pl.when(z < ZED - 1)
                def _():
                    ag(at, z - far, 0, up).start()

            @pl.when(z + far < ZED)
            def _():
                ag(at, z + far, 1, down).wait_recv()

                @pl.when(z > 0)
                def _():
                    ag(at, z + far, 1, down).start()

    def dx_part(t, i, hk):
        there = chunk_rows(i)
        krows = pl.ds(mult(deep * hk, deep), deep)
        acc = None
        for h in range(HALVES):
            term = lax.dot_general(
                gl[2 * t + h, there, :], wv[2 * t + h, krows, :],
                (((1,), (1,)), ((), ())), preferred_element_type=F32,
            )
            acc = term if acc is None else acc + term
        return acc

    def dx_step(t, i, buf):
        @pl.when((i >= HELD) | (t > 0))
        def _():
            dx_copy(t, i, buf).wait_send()

        dsend[buf] = half(dx_part(t, i, 1 - y))
        dx_copy(t, i, buf).start()
        own[buf] = dx_part(t, i, y)

    def dx_begin(t, i, buf):
        dx_copy(t, i, buf).wait_recv()
        dx_fetch(t, i).start()

    def dx_final(t, i, buf):
        @pl.when((i >= 1) | (t > 0))
        def _():
            dx_out(t, i).wait()

        dx_fetch(t, i).wait()

        def step(j, inner):
            lanes = pl.ds(mult(tile * j, tile), tile)
            dout[:, lanes] = half(own[buf, :, lanes] + wide(dfetch[:, lanes]))
            return inner

        lax.fori_loop(0, 3, step, 0)
        dx_out(t, i).start()

    def listed(u, times, do):
        e, hit = 0, False
        for index, time in enumerate(times):
            same = u == time
            e = jnp.where(same, index, e)
            hit = hit | same

        @pl.when(hit)
        def _():
            do(e)

    def chunk_of(do):
        def run(e):
            t = jnp.where(e >= n_chunk, 1, 0)
            do(t, e - n_chunk * t, lax.rem(e, HELD))

        return run

    def turn():
        lanes_at_once = min(128, tile)

        def step(q, carry):
            lanes = pl.ds(mult(q * lanes_at_once, lanes_at_once), lanes_at_once)
            xt[lanes, :] = xsrc[:, lanes].T
            return carry

        lax.fori_loop(0, tile // lanes_at_once, step, 0)

    def tile_dot(g):
        return jnp.dot(xt[...], gl[g.p], preferred_element_type=F32)

    def stage_one(g):
        tile_fetch(g.t, g.j, 1 - c, False)
        turn()
        tile_fetch(g.t, g.j, c, True)
        cstage[...] = half(tile_dot(g))
        core_copy(g).start()

    def stage_two(g):
        tile_fetch(g.t, g.j, c, False)
        turn()

        @pl.when(g.j < 2)
        def _():
            tile_fetch(g.t, g.j + 1, 1 - c, True)

        core_copy(g).wait()
        product = tile_dot(g)
        for b in range(ZED):
            block = product[:, b * hw : (b + 1) * hw] + wide(
                cland[g.buf, :, b * hw : (b + 1) * hw]
            )
            left, right = block[:, :xw], block[:, xw:]
            kept[g.trio, b] = jnp.where(x == 0, left, right)
            xstage[g.trio, b] = half(jnp.where(x == 0, right, left))

        def send(q, carry):
            across_copy(g, lax.rem(z + 3 + 3 * q, ZED)).start()
            return carry

        lax.fori_loop(0, ZED, send, 0)

    def stage_three(g):
        @pl.when(g.g >= 3)
        def _():
            for to in others:
                z_copy(g, to).wait_send()
            ax_own(g).wait_send()

        def add(b):
            across_copy(g, b).wait()
            zstage[g.trio, b] = half(kept[g.trio, b] + wide(xland[g.quad, b]))

        def step(q, carry):
            b = lax.rem(z + 3 + 3 * q, ZED)
            add(b)
            z_copy(g, b).start()
            return carry

        lax.fori_loop(0, ZED - 1, step, 0)
        add(z)
        z_own(g).start()
        ax_own(g).start()

    def stage_four(g):
        def step(q, carry):
            b = lax.rem(z + 1 + q, ZED)
            z_in(g, b).wait_recv()
            ax_copy(g, b).start()
            return carry

        lax.fori_loop(0, ZED - 1, step, 0)
        z_own(g).wait()

    def stage_five(g):
        def step(q, carry):
            b = lax.rem(z + q, ZED)
            ax_in(g, b).wait_recv()
            ac_copy(g, b).start()
            return carry

        lax.fori_loop(0, ZED, step, 0)

    def stage_six(g):
        def step(b, carry):
            ac_in(g, b).wait_recv()
            return carry

        lax.fori_loop(0, ZED, step, 0)

    def tile_of(g):
        p = lax.div(g, 3)
        t, h = tower(p)
        return Tile(
            g=g, p=p, t=t, h=h, j=g - 3 * p,
            buf=lax.rem(g, 2), trio=g - 3 * p, quad=lax.rem(g, 4),
        )

    def tile_in_hand(do):
        return lambda g: do(tile_of(g))

    def body(u, carry):
        p0 = lax.div(u, n_part)
        i0 = u - p0 * n_part
        slot0, prod0 = lax.rem(u, RING), lax.rem(u, PRODUCTS)
        buf0 = lax.rem(u, 2)

        def before(lag):
            if isinstance(lag, int):
                whole, left = divmod(lag, n_part)
            else:
                whole, left = 0, lag
            under = i0 < left
            p = p0 - whole - jnp.where(under, 1, 0)
            i = i0 - left + jnp.where(under, n_part, 0)
            in_ring = lag % RING if isinstance(lag, int) else lag
            in_prods = lag % PRODUCTS if isinstance(lag, int) else lag
            slot = slot0 - in_ring + jnp.where(slot0 < in_ring, RING, 0)
            prod = prod0 - in_prods + jnp.where(prod0 < in_prods, PRODUCTS, 0)
            t, h = tower(p)
            return Part(u=u - lag, p=p, i=i, t=t, h=h, slot=slot, prod=prod, buf=lax.rem(i, 2))

        @pl.when((u >= 5) & (u < parts + 5))
        def _():
            slot = before(5).slot
            at_place(0, ZED - 2, lambda zz: rs_up(slot, zz).wait_send())
            at_place(1, ZED - 1, lambda zz: rs_down(slot, zz).wait_send())

        @pl.when((u >= 8) & (u < parts + 8))
        def _():
            at = before(8)

            def step(b, inner):
                @pl.when((z < ZED - 1) & (b <= z))
                def _():
                    ag(at, b, 0, up).wait_send()

                @pl.when((z > 0) & (b >= z))
                def _():
                    ag(at, b, 1, down).wait_send()

                return inner

            lax.fori_loop(0, ZED, step, 0)

        ck = lax.div(i0, SUB)
        fresh = ck * SUB == i0
        t0, h0_ = tower(p0)
        xbuf = lax.rem(ck, 2)

        @pl.when((u < parts) & fresh)
        def _():
            @pl.when(i0 == 0)
            def _():
                w_own(p0).wait()
                for frm in others:
                    w_c_in(p0, frm).wait_recv()

            for copy in x_fetch(t0, ck, xbuf):
                copy.wait()

            product = jnp.dot(xc[xbuf], wv[p0], preferred_element_type=F32)
            for b in range(ZED):
                for s in range(SUB):
                    pf[prod0 + s, b] = product[
                        s * part : (s + 1) * part, b * hw : (b + 1) * hw
                    ]

        going_up = before(z)

        @pl.when((going_up.u >= 0) & (going_up.u < parts))
        def _():
            slot, prod = going_up.slot, going_up.prod
            at_place(1, ZED - 1, lambda zz: rs_from_below(slot, zz).wait_recv())

            @pl.when(z == 0)
            def _():
                for b in range(1, ZED):
                    rs[slot, b + 1] = half(pf[prod, b])

            @pl.when(z > 0)
            def _():
                def step(b, inner):
                    rs[slot, b + 1] = half(wide(rs[slot, b + 1]) + pf[prod, b])
                    return inner

                lax.fori_loop(z + 1, ZED, step, 0)

            at_place(0, ZED - 2, lambda zz: rs_up(slot, zz).start())

        going_down = before(ZED - 1 - z)

        @pl.when((going_down.u >= 0) & (going_down.u < parts))
        def _():
            slot, prod = going_down.slot, going_down.prod
            at_place(0, ZED - 2, lambda zz: rs_from_above(slot, zz).wait_recv())

            @pl.when(z == ZED - 1)
            def _():
                for b in range(ZED - 1):
                    rs[slot, b] = half(pf[prod, b])

            @pl.when(z < ZED - 1)
            def _():
                def step(b, inner):
                    rs[slot, b] = half(wide(rs[slot, b]) + pf[prod, b])
                    return inner

                lax.fori_loop(0, z, step, 0)

            at_place(1, ZED - 1, lambda zz: rs_down(slot, zz).start())

        @pl.when(fresh & (u + 2 * SUB < 2 * n_part))
        def _():
            k = p0 * n_chunk + ck + 2
            over = jnp.where(k >= n_chunk, 1, 0)
            x_copy(over, k - over * n_chunk).start()

        @pl.when(fresh & (u + SUB < parts))
        def _():
            wrap = jnp.where(ck + 1 == n_chunk, 1, 0)
            i = ck + 1 - wrap * n_chunk
            t, h = tower(p0 + wrap)

            @pl.when(h == 0)
            def _():
                x_copy(t, i).wait_recv()

            for copy in x_fetch(t, i, lax.rem(i, 2)):
                copy.start()

        @pl.when((u >= 3) & (u < parts + 3))
        def _():
            final(before(3), before(2))

        forward_ag(before(4), 1)
        forward_ag(before(5), 2)
        forward_ag(before(6), 3)

        listed(u, DX_BEGINS, chunk_of(dx_begin))
        listed(u, DX_ENDS, chunk_of(dx_final))
        listed(u, DX_TIMES, chunk_of(dx_step))

        listed(u, THREES, tile_in_hand(stage_three))
        listed(u, TWOS, tile_in_hand(stage_two))
        listed(u, ONES, tile_in_hand(stage_one))
        listed(u, FOURS, tile_in_hand(stage_four))
        listed(u, FIVES, tile_in_hand(stage_five))
        listed(u, SIXES, tile_in_hand(stage_six))

        def first_fetch(p):
            tile_fetch(lax.div(p, HALVES), 0, 1 - c, True)

        listed(u, [time - 1 for time in ONES[::3]], first_fetch)

        for p, times in W_STRIPS.items():
            def send_strip(r, p=p):
                for to in others:
                    w_z_strip(p, to, r).start()

                @pl.when(r == 0)
                def _():
                    w_own(p).start()

            listed(u, times, send_strip)

        for p, times in W_ACROSS.items():
            for q, time in enumerate(times):
                @pl.when(u == time)
                def _(p=p, q=q):
                    w_z_in(p, others[q]).wait_recv()
                    w_x(p, others[q]).start()

        for p, times in W_CORES.items():
            for q, time in enumerate(times):
                @pl.when(u == time)
                def _(p=p, q=q):
                    w_x_in(p, others[q]).wait_recv()
                    w_c(p, others[q]).start()

        @pl.when(u == parts + 3)
        def _():
            for p in range(PHASES):
                t, h = p // HALVES, p % HALVES
                for s in range(2):
                    for what in range(2):
                        sums[0, pl.ds(4 * what + 2 * s + t, 1), h * hw : (h + 1) * hw] = jnp.sum(
                            stat[p, 2 * what + s], axis=0, keepdims=True
                        )
            sum_copy(0, across_c).start()

        @pl.when(u == parts + 4)
        def _():
            sum_copy(0, across_c).wait()
            sums[1] = sums[0] + sums_land[0]
            sum_copy(1, across_x).start()

        @pl.when(u == parts + 5)
        def _():
            sum_copy(1, across_x).wait()
            both = sums[1] + sums_land[1]
            sums[2] = both
            member = (
                lax.broadcasted_iota(jnp.int32, (width, lane), 0) % FLAG_GROUPS
                == lax.broadcasted_iota(jnp.int32, (width, lane), 1) % FLAG_GROUPS
            ).astype(F32)
            bias_rows = both[0:4]
            inner = both[0:2] * both[2:4]
            stack = jnp.concatenate([inner, bias_rows * bias_rows, inner], axis=0)
            prods[0] = jnp.dot(
                stack, member, precision=lax.Precision.HIGHEST, preferred_element_type=F32
            )
            prod_y().start()

        @pl.when(u == parts + 6)
        def _():
            prod_y().wait()
            prods[1] = prods[0] + prods_land[ZED]
            for to in others:
                prod_z(to).start()

        @pl.when(u == parts + 7)
        def _():
            for frm in others:
                prod_z_in(frm).wait_recv()
            prods_land[z] = prods[1]
            whole = prods_land[0] + prods_land[1] + prods_land[2] + prods_land[3]
            both = sums[2]
            group = lax.broadcasted_iota(jnp.int32, (1, lane), 1) % FLAG_GROUPS

            def over(row):
                return jnp.concatenate([row] * (width // lane), axis=1)

            def flag_row(s, t):
                row = jnp.zeros((1, lane), F32)
                for g in range(FLAG_GROUPS):
                    row = jnp.where(group == g, flags[s, t, g].astype(F32), row)
                return row

            for t in range(2):
                task0, task1 = both[t : t + 1], both[2 + t : 3 + t]
                dots = whole[t : t + 1]
                coef0 = over(flag_row(0, t) * dots / (whole[4 + t : 5 + t] + 1e-06))
                coef1 = over(flag_row(1, t) * dots / (whole[2 + t : 3 + t] + 1e-06))
                gbias[t : t + 1] = (task0 - coef0 * task1) + (task1 - coef1 * task0)
            for s in range(2):
                gstitch[s] = both[4 + 2 * s : 6 + 2 * s]

        return carry

    lax.fori_loop(0, max(SIXES + DX_ENDS) + 1, body, 0)

    last = 3 * PHASES - 1

    for g in (last - 2, last - 1, last):
        for to in others:
            z_copy(tile_of(g), to).wait_send()
        ax_own(tile_of(g)).wait_send()
    for i in range(n_chunk - HELD, n_chunk):
        dx_copy(1, i, (n_chunk + i) % HELD).wait_send()
    for i in (n_part - 2, n_part - 1):
        mixed_out(1, i, i % 2).wait()
    dx_out(1, n_chunk - 1).wait()

    def drain_tiles(g, carry):
        at = tile_of(g)
        for b in others:
            ax_copy(at, b).wait_send()
        for b in range(ZED):
            ac_copy(at, b).wait_send()
        return carry

    lax.fori_loop(0, last + 1, drain_tiles, 0)

    def drain_x(i, carry):
        x_copy(0, i).wait_send()
        x_copy(1, i).wait_send()
        return carry

    lax.fori_loop(0, n_chunk, drain_x, 0)

    def drain_w(p, carry):
        for to in others:
            w_z(p, to).wait_send()
            w_x(p, to).wait_send()
            w_c(p, to).wait_send()
        return carry

    lax.fori_loop(0, PHASES, drain_w, 0)
    for to in others:
        prod_z(to).wait_send()


def fused_call(feat, wts, cot, bias, stitch, counts, mask, flags):
    rows, deep, width = feat.shape[1], feat.shape[2], wts.shape[2]
    chunk = rows // 6
    part = chunk // SUB
    hw, kz, tile = width // 2, 2 * deep, deep // 3
    cat, xw = 4 * hw, width // 4
    lane = min(128, width)
    dma = pltpu.SemaphoreType.DMA
    anywhere = pl.BlockSpec(memory_space=pl.ANY)
    inside = pl.BlockSpec(memory_space=pltpu.VMEM)
    scalars = pl.BlockSpec(memory_space=pltpu.SMEM)

    def v(shape, kind=BF16):
        return pltpu.VMEM(shape, kind)

    out_shape = [
        jax.ShapeDtypeStruct((2, rows, width), BF16),
        jax.ShapeDtypeStruct((2, rows, deep), BF16),
        jax.ShapeDtypeStruct((2, ZED, kz, width), BF16),
        jax.ShapeDtypeStruct((2, width), F32),
        jax.ShapeDtypeStruct((2, 2, width), F32),
        jax.ShapeDtypeStruct((2, rows, deep), BF16),
        jax.ShapeDtypeStruct((2, rows, deep), BF16),
    ]
    scratch = [
        v((PHASES, kz, cat)),
        v((PHASES, rows, cat)),
        v((RING, 5, part, hw)),
        v((2, rows, hw), F32),
        v((2, chunk, kz)),
        v((PRODUCTS, ZED, part, hw), F32),
        v((2, 2, part, hw)),
        v((2, 2, part, hw)),
        v((HELD, chunk, deep), F32),
        v((HELD, chunk, deep)),
        v((chunk, deep)),
        v((chunk, deep)),
        v((rows, tile)),
        v((tile, rows)),
        v((tile, cat)),
        v((2, tile, cat)),
        v((3, ZED, tile, xw)),
        v((4, ZED, tile, xw)),
        v((3, ZED, tile, xw), F32),
        v((3, ZED, tile, xw)),
        v((rows, lane), F32),
        v((PHASES, 4, 8, hw), F32),
        v((3, 8, width), F32),
        v((2, 8, width), F32),
        v((2, 8, lane), F32),
        v((5, 8, lane), F32),
        dma((RING, 2)), dma((RING, 2)), dma((RING, 8)), dma((RING, 4)),
        dma((12,)), dma((12,)),
        dma((4, 4)), dma((4, 4)), dma((4, 4)), dma((4, 4)), dma((4, 4)), dma((4, 4)), dma((4,)),
        dma((2, 2)), dma((2,)), dma((2,)), dma((HELD,)), dma((12,)), dma((1,)), dma((1,)),
        dma((1,)), dma((1,)), dma((2,)), dma((3, 4)), dma((4, 4)), dma((3, 4)), dma((12, 4)),
        dma((3,)), dma((3,)),
        dma((12, 4)), dma((12, 4)), dma((12, 4)), dma((12, 4)), dma((8,)), dma((8,)),
    ]
    flops = 3 * 2 * 2 * rows * kz * cat * 2
    return pl.pallas_call(
        functools.partial(fused_kernel, rows, deep, width, chunk),
        out_shape=out_shape,
        in_specs=[anywhere] * 3 + [inside] * 4 + [scalars],
        out_specs=[anywhere] * 3 + [inside] * 2 + [anywhere] * 2,
        scratch_shapes=scratch,
        compiler_params=pltpu.CompilerParams(
            collective_id=0, has_side_effects=True, vmem_limit_bytes=64 * 1024 * 1024
        ),
        cost_estimate=pl.CostEstimate(
            flops=flops, bytes_accessed=200_000_000, transcendentals=2 * rows * width * 2
        ),
        name="cross_stitch_step",
    )(feat, wts, cot, bias, stitch, counts, mask, flags)


def finish_kernel(
    block, low, mixed, gfeat, gbias, gstitch,
    out, mixed_out, gfeat_out, gbias_out, gstitch_out,
    taken, given, held_mixed, held_gfeat, in_sem, out_sem, pass_sem,
):
    n_block = low.shape[0] // block
    fetched = (
        pltpu.make_async_copy(mixed, held_mixed, pass_sem.at[0]),
        pltpu.make_async_copy(gfeat, held_gfeat, pass_sem.at[1]),
    )
    passed = (
        pltpu.make_async_copy(held_mixed, mixed_out, pass_sem.at[2]),
        pltpu.make_async_copy(held_gfeat, gfeat_out, pass_sem.at[3]),
    )

    def take(i):
        return pltpu.make_async_copy(
            low.at[pl.ds(i * block, block)], taken.at[i % WIDEN_SLOTS], in_sem.at[i % WIDEN_SLOTS]
        )

    def give(i):
        return pltpu.make_async_copy(
            given.at[i % WIDEN_SLOTS], out.at[pl.ds(i * block, block)], out_sem.at[i % WIDEN_SLOTS]
        )

    for i in range(min(WIDEN_SLOTS, n_block)):
        take(i).start()
    for copy in fetched:
        copy.start()
    gbias_out[...] = gbias[...]
    gstitch_out[...] = gstitch[...]
    for i in range(n_block):
        slot = i % WIDEN_SLOTS
        take(i).wait()
        if i >= WIDEN_SLOTS:
            give(i - WIDEN_SLOTS).wait()
        given[slot] = wide(taken[slot])
        give(i).start()
        if i + WIDEN_SLOTS < n_block:
            take(i + WIDEN_SLOTS).start()
        if i == 2:
            for arrived, copy in zip(fetched, passed):
                arrived.wait()
                copy.start()
    for i in range(max(0, n_block - WIDEN_SLOTS), n_block):
        give(i).wait()
    for copy in passed:
        copy.wait()


def finish(low, mixed, gfeat, gbias, gstitch):
    tall, width = low.shape
    block = tall // WIDEN_BLOCKS
    anywhere = pl.BlockSpec(memory_space=pl.ANY)
    inside = pl.BlockSpec(memory_space=pltpu.VMEM)
    moved = sum(a.size * a.dtype.itemsize for a in (mixed, gfeat))
    return pl.pallas_call(
        functools.partial(finish_kernel, block),
        in_specs=[anywhere] * 3 + [inside] * 2,
        out_specs=[anywhere] * 3 + [inside] * 2,
        out_shape=[
            jax.ShapeDtypeStruct(a.shape, kind)
            for a, kind in ((low, F32), (mixed, BF16), (gfeat, BF16), (gbias, F32), (gstitch, F32))
        ],
        scratch_shapes=[
            pltpu.VMEM((WIDEN_SLOTS, block, width), BF16),
            pltpu.VMEM((WIDEN_SLOTS, block, width), F32),
            pltpu.VMEM(mixed.shape, BF16),
            pltpu.VMEM(gfeat.shape, BF16),
            pltpu.SemaphoreType.DMA((WIDEN_SLOTS,)),
            pltpu.SemaphoreType.DMA((WIDEN_SLOTS,)),
            pltpu.SemaphoreType.DMA((4,)),
        ],
        compiler_params=pltpu.CompilerParams(vmem_limit_bytes=60 * 1024 * 1024),
        cost_estimate=pl.CostEstimate(
            flops=tall * width, bytes_accessed=6 * tall * width + 2 * moved, transcendentals=0
        ),
        name="finish",
    )(low, mixed, gfeat, gbias, gstitch)


def fused_plan(mesh):
    def per_device(features, weights, bias, stitch, cotangent, crop_counts, row_mask, flags):
        rows, deep = features.shape[1:]
        width = weights.shape[2]
        mixed, gfeat, gwt, gbias, gstitch, _, _ = fused_call(
            features, weights, cotangent, bias, stitch,
            crop_counts.reshape(1, -1), row_mask.reshape(-1, min(128, rows // 6)), flags,
        )
        grad_weights, mixed, gfeat, gbias, gstitch = finish(
            gwt.reshape(-1, width), mixed, gfeat, gbias, gstitch
        )
        return mixed, gfeat, grad_weights.reshape(2, ZED * 2 * deep, width), gbias, gstitch

    return per_device


def plan_for(mesh):
    if mesh.shape["batch"] == 4 and mesh.shape["mp"] == 2 * ZED:
        return fused_plan(mesh)
    return generic_plan(mesh)


def solution(mesh):
    in_specs = (
        P(None, "batch", "mp"),
        P(None, None, "mp"),
        P(None, "mp"),
        P(None, None, "mp"),
        P(None, "batch", "mp"),
        P("batch"),
        P("batch"),
        P(),
    )
    out_specs = (
        P(None, "batch", "mp"),
        P(None, "batch", "mp"),
        P(None, None, "mp"),
        P(None, "mp"),
        P(None, None, "mp"),
    )
    return jax.shard_map(
        plan_for(mesh), mesh=mesh, in_specs=in_specs, out_specs=out_specs, check_vma=False
    )
```

profile of v0, /device:TPU:0, one launch (start us, length us, event | category | flops | bytes accessed | tf_op | source)
XLA Modules:
  0.0 560.8 jit_solution(16743384399626346538)
XLA Ops:
  0.6 534.4 %cross_stitch_step.1 = (bf16[2,1536,512]{2,1,0:T(8,128)(2,1)}, bf16[2,1536,1152]{2,1,0:T(8,128)(2,1)}, bf16[2,4,2304,512]{3,2,1,0:T(8,128)(2,1)}, f32[2,512]{1,0...) custom-call(bf16[2,1536,1152]{2,1,0:T(8,128)(2,1)} %feat.1, ...), custom_call_target="tpu_custom_call" | custom-call | flops 86973087744 | bytes 200000000 | tf_op jit(solution)/shard_map/cross_stitch_step/pallas_call | solution.py:1094
  535.0 25.8 %finish.1 = (f32[18432,512]{1,0:T(8,128)}, bf16[2,1536,512]{2,1,0:T(8,128)(2,1)}, bf16[2,1536,1152]{2,1,0:T(8,128)(2,1)}, f32[2,512]{1,0:T(2,128)}, f32[2,2,512]{2,1,0:T(2,128)}) custom-call(bf16[18432,512]{1,0:T(8,128)(2,1)} %bitcast.4, bf16[2,1536,512]{2,1,0:T(8,128)(2,1)} %get-tuple-element.16.mixed, bf16[2,1536,1152]{2,1,0:T(8,128)(2,1)} %get-tuple-element.17.gfeat, ...), custom_call_target="tpu_custom_call" | custom-call | flops 9437184 | bytes 77070336 | tf_op jit(solution)/shard_map/finish/pallas_call | solution.py:1166
where the time goes:
time: 562 us; the launch traced here: 561 us
  Pallas kernels  560 us (100%)
    pallas_call x1, Pallas kernels, fused_call(): pl.pallas_call(functools.partial(fused_kernel, rows, deep, width, chunk),...  534 us
    pallas_call x1, Pallas kernels, finish(): pl.pallas_call(functools.partial(finish_kernel, block), in_specs=[anywher...  25.8 us

commit v1 on v0

--- a/solution.py
+++ b/solution.py
@@ -133,8 +133,8 @@
 SUB = 2
 PRODUCTS = 6
 HELD = 4
-WIDEN_BLOCKS = 18
-WIDEN_SLOTS = 6
+WIDEN_BLOCKS = 12
+WIDEN_SLOTS = 4
 
 DX_TIMES = (20, 21, 23, 25, 27, 29, 43, 45, 48, 50, 58, 64)
 DX_BEGINS = (22, 24, 26, 28, 30, 34, 44, 48, 57, 60, 68, 76)
@@ -145,7 +145,7 @@
 FOURS = (25, 30, 35, 37, 44, 47, 50, 54, 60, 67, 68, 73)
 FIVES = (33, 36, 44, 45, 51, 59, 62, 67, 74, 76, 82, 85)
 SIXES = (35, 43, 47, 57, 64, 70, 75, 82, 84, 86, 87, 90)
-W_STRIPS = {2: (5, 7, 8, 11, 12, 13), 3: (21, 22, 23, 24, 26, 27)}
+W_STRIPS = {2: (5, 7, 8, 11, 12, 13), 3: (19, 21, 23, 25, 26, 27)}
 W_ACROSS = {1: (0, 0, 2), 2: (16, 21, 22), 3: (29, 29, 34)}
 W_CORES = {1: (1, 6, 7), 2: (21, 23, 23), 3: (33, 33, 35)}
 

time: 562 us -> 563 us (level)
  no operation moved by 1% of the time
where the time goes in v1:
time: 563 us; the launch traced here: 562 us
  Pallas kernels  561 us (100%)
    pallas_call x1, Pallas kernels, fused_call(): pl.pallas_call(functools.partial(fused_kernel, rows, deep, width, chunk),...  536 us
    pallas_call x1, Pallas kernels, finish(): pl.pallas_call(functools.partial(finish_kernel, block), in_specs=[anywher...  25.6 us

profile of v1, /device:TPU:0, one launch (start us, length us, event | category | flops | bytes accessed | tf_op | source)
XLA Modules:
  0.0 562.1 jit_solution(15602091833504658864)
XLA Ops:
  0.6 535.9 %cross_stitch_step.1 = (bf16[2,1536,512]{2,1,0:T(8,128)(2,1)}, bf16[2,1536,1152]{2,1,0:T(8,128)(2,1)}, bf16[2,4,2304,512]{3,2,1,0:T(8,128)(2,1)}, f32[2,512]{1,0...) custom-call(bf16[2,1536,1152]{2,1,0:T(8,128)(2,1)} %feat.1, ...), custom_call_target="tpu_custom_call" | custom-call | flops 86973087744 | bytes 200000000 | tf_op jit(solution)/shard_map/cross_stitch_step/pallas_call | solution.py:1094
  536.5 25.6 %finish.1 = (f32[18432,512]{1,0:T(8,128)}, bf16[2,1536,512]{2,1,0:T(8,128)(2,1)}, bf16[2,1536,1152]{2,1,0:T(8,128)(2,1)}, f32[2,512]{1,0:T(2,128)}, f32[2,2,512]{2,1,0:T(2,128)}) custom-call(bf16[18432,512]{1,0:T(8,128)(2,1)} %bitcast.4, bf16[2,1536,512]{2,1,0:T(8,128)(2,1)} %get-tuple-element.16.mixed, bf16[2,1536,1152]{2,1,0:T(8,128)(2,1)} %get-tuple-element.17.gfeat, ...), custom_call_target="tpu_custom_call" | custom-call | flops 9437184 | bytes 77070336 | tf_op jit(solution)/shard_map/finish/pallas_call | solution.py:1166
